TPU v7x, 512 devices: a whole 4x4x16 slice. The times are simulated.
512 devices in a mesh: doc: 64 (over y, z), bin: 8 (over x, core).
Axes of the slice: x: 4, y: 4, z: 16, core: 2. Of those that a mesh axis runs over, the one named last changes fastest.
Arguments:
- profiles: float32 [8192, 8192], P('doc', 'bin'), may hold values from -6 to 6
- assign: int32 [8192], P('doc'), may hold values from 0 to 4095, as said below
Outputs:
- centroids: float32 [8, 512, 8192], P('bin', 'doc')
- scores: float32 [4096, 8192], P('bin', 'doc')
Inputs may be any that keep to these rules, and one draw needn't show every extreme that they name: `assign`: cluster k belongs to owner (k % 512) // 8. In each aligned block of 128 documents, at most 8 documents are assigned to the clusters of one owner, and some owner has exactly 8 of them.
All inputs are finite; a program needn't handle non-finite values.
Results may differ from a plain program's by a relative error of at most 0.0029.
Values may be sent and summed in bfloat16 or wider, within the bound.
A program may use at most 64 MiB of HBM per device.

v0:
```python
import jax
import jax.numpy as jnp
from jax import lax
from jax.sharding import PartitionSpec as P

K = 4096
norm_epsilon = 1e-06


def shards(profiles, assign):
    doc_devs = lax.axis_size("doc")
    bin_devs = lax.axis_size("bin")
    doc_count, slab_width = profiles.shape
    slice_width = K // bin_devs
    part_width = slice_width // doc_devs
    owned_count = part_width * bin_devs
    capacity = 4 * doc_count // doc_devs
    owner_rank = assign % slice_width // part_width
    local_index = assign // slice_width * part_width + assign % part_width
    owner_hits = (owner_rank[:, None] == jnp.arange(doc_devs, dtype=jnp.int32)[None, :]).astype(
        jnp.int32
    )
    slot_rank = jnp.sum(jnp.cumsum(owner_hits, axis=0) * owner_hits, axis=1) - 1
    slot_index = owner_rank * capacity + slot_rank
    send_rows = (
        jnp.zeros((doc_devs * capacity, slab_width), jnp.float32).at[slot_index].set(profiles)
    )
    send_ids = jnp.full((doc_devs * capacity,), -1, jnp.int32).at[slot_index].set(local_index)
    send_rows = send_rows.reshape(doc_devs, capacity, slab_width)
    send_ids = send_ids.reshape(doc_devs, capacity)
    got_rows, got_ids = (
        lax.all_to_all(send_rows, "doc", split_axis=0, concat_axis=0, tiled=True),
        lax.all_to_all(send_ids, "doc", split_axis=0, concat_axis=0, tiled=True),
    )
    member = (
        got_ids.reshape(-1)[None, :] == jnp.arange(owned_count, dtype=jnp.int32)[:, None]
    ).astype(jnp.float32)
    cluster_sums = jnp.dot(
        member,
        got_rows.reshape(-1, slab_width),
        precision=lax.Precision.HIGHEST,
        preferred_element_type=jnp.float32,
    )
    cluster_sums = cluster_sums.reshape(bin_devs, part_width, slab_width)
    partial_squares = jnp.sum(cluster_sums * cluster_sums, axis=2)
    total_squares = lax.psum(partial_squares, "bin")
    unit = cluster_sums * lax.rsqrt(total_squares + norm_epsilon)[:, :, None]
    centroids = lax.all_to_all(unit, "bin", split_axis=0, concat_axis=2, tiled=True)
    gathered = lax.all_gather(unit.astype(jnp.bfloat16), "doc", axis=1, tiled=True)
    panel_rows = gathered.reshape(-1, slab_width)
    doc_values = profiles.astype(jnp.bfloat16)
    scores = lax.psum_scatter(
        lax.dot_general(
            panel_rows, doc_values, (((1,), (1,)), ((), ())), preferred_element_type=jnp.float32
        ),
        "bin",
        scatter_dimension=0,
        tiled=True,
    )
    return (centroids, scores)


def solution(mesh):
    in_specs = (P("doc", "bin"), P("doc"))
    out_specs = (P("bin", "doc", None), P("bin", "doc"))
    return jax.shard_map(shards, mesh=mesh, in_specs=in_specs, out_specs=out_specs, check_vma=False)
```

profile of v0, /device:TPU:8, one launch (start us, length us, event | category | flops | bytes accessed | tf_op | source)
XLA Modules:
  0.0 360.2 jit_solution(9232095160435295296)
XLA Ops:
  7.2 0.7 fusion.12
  7.8 0.1 fusion.9
  7.9 0.2 reduce_window_sum.11
  8.1 0.2 select_reduce_fusion
  8.3 1.0 scatter_custom_fusion
  9.3 0.7 all_to_all.22
  10.0 18.7 %all-to-all-start = ((s32[64,1,8]{2,1,0:T(1,128)}), s32[64,1,8]{2,1,0:T(1,128)S(1)}, u32[]{:S(2)}, u32[]{:S(2)}) async-start(s32[64,1,8]{2,1,0:T(1,128)} %bitcast), calls=%async_computation | async-start | bytes 65536 | tf_op jit(solution)/shard_map/all_to_all | solution.py:33
  28.7 3.0 scatter_custom_fusion.1
  31.7 10.5 %all-to-all-done = s32[64,1,8]{2,1,0:T(1,128)S(1)} async-done(((s32[64,1,8]{2,1,0:T(1,128)}), s32[64,1,8]{2,1,0:T(1,128)S(1)}, u32[]{:S(2)}, u32[]{:S(2)}) %all-to-all-start) | async-done | bytes 2080 | tf_op jit(solution)/shard_map/all_to_all | solution.py:33
  42.2 5.6 %all-to-all-start.1 = ((f32[64,8,1024]{2,1,0:T(8,128)}), f32[64,8,1024]{2,1,0:T(8,128)S(1)}, u32[]{:S(2)}, u32[]{:S(2)}) async-start(f32[64,8,1024]{2,1,0:T(8,128)} %bitcast.1), calls=%async_computation.1 | async-start | bytes 4194304 | tf_op jit(solution)/shard_map/all_to_all | solution.py:32
  47.8 0.0 copy-start
  47.8 0.0 all-gather.2.cloned.1.call-start
  47.8 0.5 broadcast.71
  48.3 0.7 reduce.3
  49.1 0.1 eq.45
  49.2 95.7 %all-to-all-done.1 = f32[64,8,1024]{2,1,0:T(8,128)S(1)} async-done(((f32[64,8,1024]{2,1,0:T(8,128)}), f32[64,8,1024]{2,1,0:T(8,128)S(1)}, u32[]{:S(2)}, u32[]{:S(2)}) %all-to-all-start.1) | async-done | bytes 2097184 | tf_op jit(solution)/shard_map/all_to_all | solution.py:32
  144.9 1.0 multiply_reduce_fusion
  145.9 12.4 %psum.7 = f32[8,8]{1,0:T(8,128)S(1)} all-reduce(f32[8,8]{1,0:T(8,128)S(1)} %get-tuple-element.6), channel_id=1, replica_groups=mesh['doc'=64,'bin'=8] {'bin'}, use_global_device_ids=true, to_apply=%region_5.6 | all-reduce | flops 64 | bytes 512 | tf_op jit(solution)/shard_map/psum | solution.py:46
  158.3 0.8 fusion.13
  159.1 0.0 all-gather.2.cloned.1.call-update
  159.1 0.0 reduce-scatter.2.cloned.1.call-start
  159.2 149.0 %all-gather.2.cloned.1.call-done = bf16[8,512,1024]{2,1,0:T(8,128)(2,1)} async-done(((bf16[8,8,1024]{2,1,0:T(8,128)(2,1)}), bf16[8,512,1024]{2,1,0:T(8,128)(2,1)}) %all-gather.2.cloned.1.call-update) | async-done | bytes 8388624 | tf_op jit(solution)/shard_map/all_gather | solution.py:49
  308.1 0.0 copy-done
  308.1 7.1 %fusion.4 = f32[4096,128]{1,0:T(8,128)} fusion(bf16[4096,1024]{1,0:T(8,128)(2,1)} %bitcast.18, f32[128,1024]{1,0:T(8,128)S(1)} %copy-done), kind=kOutput, calls=%fused_computation.6 | convolution fusion | flops 1073872896 | bytes 11010048 | tf_op jit(solution)/shard_map/dot_general | solution.py:53
  315.2 0.0 reduce-scatter.2.cloned.1.call-update
  315.3 11.6 %all_to_all.32 = f32[8,8,1024]{2,1,0:T(8,128)S(1)} all-to-all(f32[8,8,1024]{2,1,0:T(8,128)S(1)} %get-tuple-element.3), channel_id=1, replica_groups=mesh['doc'=64,'bin'=8] {'bin'}, dimensions={0} | all-to-all | bytes 524288 | tf_op jit(solution)/shard_map/all_to_all | solution.py:48
  326.9 25.8 %reduce-scatter.2.cloned.1.call-done = f32[512,128]{1,0:T(8,128)} async-done(((f32[4096,128]{1,0:T(8,128)}), f32[512,128]{1,0:T(8,128)}) %reduce-scatter.2.cloned.1.call-update) | async-done | bytes 262160 | tf_op jit(solution)/shard_map/reduce_scatter | solution.py:52
  352.7 0.7 copy.6
  (3 shorter events, 0.0 us)
Async XLA Ops:
  10.0 32.2 %all-to-all-start = ((s32[64,1,8]{2,1,0:T(1,128)}), s32[64,1,8]{2,1,0:T(1,128)S(1)}, u32[]{:S(2)}, u32[]{:S(2)}) async-start(s32[64,1,8]{2,1,0:T(1,128)} %bitcast), calls=%async_computation | async-start | bytes 65536 | tf_op jit(solution)/shard_map/all_to_all | solution.py:33
  42.2 102.7 %all-to-all-start.1 = ((f32[64,8,1024]{2,1,0:T(8,128)}), f32[64,8,1024]{2,1,0:T(8,128)S(1)}, u32[]{:S(2)}, u32[]{:S(2)}) async-start(f32[64,8,1024]{2,1,0:T(8,128)} %bitcast.1), calls=%async_computation.1 | async-start | bytes 4194304 | tf_op jit(solution)/shard_map/all_to_all | solution.py:32
  47.8 260.4 %copy-start = (f32[128,1024]{1,0:T(8,128)S(1)}, f32[128,1024]{1,0:T(8,128)}, u32[]{:S(2)}) copy-start(f32[128,1024]{1,0:T(8,128)} %param.2) | copy-start | bytes 1572868
  47.8 260.3 %all-gather.2.cloned.1.call-start = ((), (), s32[]{:S(2)}) async-start(), calls=%async_computation.4 | async-start | bytes 8519680 | tf_op jit(solution)/shard_map/all_gather | solution.py:49
  159.1 193.6 %reduce-scatter.2.cloned.1.call-start = ((), (), s32[]{:S(2)}) async-start(), calls=%async_computation.5 | async-start | bytes 2359296 | tf_op jit(solution)/shard_map/reduce_scatter | solution.py:52
Sparse Core Ops, SparseCore 0:
  159.2 148.8 all-gather.1
  315.4 37.2 reduce-scatter.1
where the time goes:
time: 361 us; the launch traced here: 360 us
  waiting for transfers between devices  281 us (78%)
  starting transfers between devices  24.4 us (7%)
  blocking collectives  24 us (7%)
  between operations  14.1 us (4%)
  matrix products  8.16 us (2%)
  local copies, waits for them, and re-layouts  5.95 us (2%)
    all_gather x1, waiting for transfers between devices, shards(): lax.all_gather(unit.astype(jnp.bfloat16), 'doc', axis=1, tiled=True)  149 us
    all_to_all x1, waiting for transfers between devices, shards(): lax.all_to_all(send_rows, 'doc', split_axis=0, concat_axis=0, tiled=True)  95.7 us
    reduce_scatter x1, waiting for transfers between devices, shards(): lax.psum_scatter(lax.dot_general(panel_rows, doc_values, (((1,), (1,)), (...  25.8 us
    all_to_all x1, starting transfers between devices, shards(): lax.all_to_all(send_ids, 'doc', split_axis=0, concat_axis=0, tiled=True)  18.7 us
    psum x1, blocking collectives, shards(): total_squares = lax.psum(partial_squares, 'bin')  12.4 us
    all_to_all x1, blocking collectives, shards(): lax.all_to_all(unit, 'bin', split_axis=0, concat_axis=2, tiled=True)  11.6 us
    all_to_all x1, waiting for transfers between devices, shards(): lax.all_to_all(send_ids, 'doc', split_axis=0, concat_axis=0, tiled=True)  10.5 us
  transfers between devices with their start and end apart: 4, of which 4 were waited for; matrix products, arithmetic and copies ran while one was open for 1% of the time, Pallas kernels for 0%

commit v1 on v0

--- a/solution.py
+++ b/solution.py
@@ -46,7 +46,11 @@
     total_squares = lax.psum(partial_squares, "bin")
     unit = cluster_sums * lax.rsqrt(total_squares + norm_epsilon)[:, :, None]
     centroids = lax.all_to_all(unit, "bin", split_axis=0, concat_axis=2, tiled=True)
-    gathered = lax.all_gather(unit.astype(jnp.bfloat16), "doc", axis=1, tiled=True)
+    block = unit.astype(jnp.bfloat16)
+    devices = lax.axis_size("doc")
+    blocks = jnp.stack([block for _ in range(devices)])
+    blocks = lax.all_to_all(blocks, "doc", split_axis=0, concat_axis=0)
+    gathered = jnp.concatenate(blocks, axis=1)
     panel_rows = gathered.reshape(-1, slab_width)
     doc_values = profiles.astype(jnp.bfloat16)
     scores = lax.psum_scatter(

time: 361 us -> 591 us (1.64)
  blocking collectives: 24 us -> 397 us
  waiting for transfers between devices: 281 us -> 130 us
  local copies, waits for them, and re-layouts: 5.95 us -> 15.1 us
    all_to_all x0 -> x1, blocking collectives: none -> 375 us  [shards(): blocks = lax.all_to_all(blocks, 'doc', split_axis=0, concat_axis=0)]
    all_gather x1 -> x0, waiting for transfers between devices: 149 us -> none  [shards(): lax.all_gather(unit.astype(jnp.bfloat16), 'doc', axis=1, tiled=True)]
    all_to_all x0 -> x1, local copies, waits for them, and re-layouts: none -> 8.06 us  [shards(): blocks = lax.all_to_all(blocks, 'doc', split_axis=0, concat_axis=0)]
  transfers between devices with their start and end apart: 4 -> 3, of which waited for: 4 -> 3; matrix products, arithmetic and copies ran while one was open for 1% -> 1% of each run, Pallas kernels for 0% -> 0%
where the time goes in v1:
time: 591 us
  blocking collectives  397 us (67%)
  waiting for transfers between devices  130 us (22%)
  starting transfers between devices  24.4 us (4%)
  local copies, waits for them, and re-layouts  15.1 us (3%)
  between operations  14.1 us (2%)
  matrix products  8.16 us (1%)
    all_to_all x1, blocking collectives, shards(): blocks = lax.all_to_all(blocks, 'doc', split_axis=0, concat_axis=0)  375 us
    all_to_all x1, waiting for transfers between devices, shards(): lax.all_to_all(send_rows, 'doc', split_axis=0, concat_axis=0, tiled=True)  95.7 us
    reduce_scatter x1, waiting for transfers between devices, shards(): lax.psum_scatter(lax.dot_general(panel_rows, doc_values, (((1,), (1,)), (...  23.8 us
    all_to_all x1, starting transfers between devices, shards(): lax.all_to_all(send_ids, 'doc', split_axis=0, concat_axis=0, tiled=True)  18.7 us
    psum x1, blocking collectives, shards(): total_squares = lax.psum(partial_squares, 'bin')  12.4 us
  transfers between devices with their start and end apart: 3, of which 3 were waited for; matrix products, arithmetic and copies ran while one was open for 1% of the time, Pallas kernels for 0%

profile of v1, /device:TPU:8, one launch (start us, length us, event | category | flops | bytes accessed | tf_op | source)
XLA Modules:
  0.0 591.0 jit_solution(4196521914417750470)
XLA Ops:
  7.2 0.7 fusion.12
  7.8 0.1 fusion.9
  7.9 0.2 reduce_window_sum.11
  8.1 0.2 select_reduce_fusion
  8.3 1.0 scatter_custom_fusion
  9.3 0.7 all_to_all.25
  10.0 18.7 %all-to-all-start = ((s32[64,1,8]{2,1,0:T(1,128)}), s32[64,1,8]{2,1,0:T(1,128)S(1)}, u32[]{:S(2)}, u32[]{:S(2)}) async-start(s32[64,1,8]{2,1,0:T(1,128)} %bitcast), calls=%async_computation | async-start | bytes 65536 | tf_op jit(solution)/shard_map/all_to_all | solution.py:33
  28.7 3.0 scatter_custom_fusion.1
  31.7 10.5 %all-to-all-done = s32[64,1,8]{2,1,0:T(1,128)S(1)} async-done(((s32[64,1,8]{2,1,0:T(1,128)}), s32[64,1,8]{2,1,0:T(1,128)S(1)}, u32[]{:S(2)}, u32[]{:S(2)}) %all-to-all-start) | async-done | bytes 2080 | tf_op jit(solution)/shard_map/all_to_all | solution.py:33
  42.2 5.6 all-to-all-start.1
  47.8 0.0 reduce-scatter.2.cloned.1.call-start
  47.8 0.5 broadcast.73
  48.3 0.7 reduce.3
  49.1 0.1 eq.45
  49.1 95.7 %all-to-all-done.1 = f32[64,8,1024]{2,1,0:T(8,128)S(1)} async-done(((f32[64,8,1024]{2,1,0:T(8,128)}), f32[64,8,1024]{2,1,0:T(8,128)S(1)}, u32[]{:S(2)}, u32[]{:S(2)}) %all-to-all-start.1) | async-done | bytes 2097184 | tf_op jit(solution)/shard_map/all_to_all | solution.py:32
  144.9 1.0 multiply_reduce_fusion
  145.9 12.4 %psum.7 = f32[8,8]{1,0:T(8,128)S(1)} all-reduce(f32[8,8]{1,0:T(8,128)S(1)} %get-tuple-element.6), channel_id=1, replica_groups=mesh['doc'=64,'bin'=8] {'bin'}, use_global_device_ids=true, to_apply=%region_5.6 | all-reduce | flops 64 | bytes 512 | tf_op jit(solution)/shard_map/psum | solution.py:46
  158.3 0.1 fusion.13
  158.4 1.1 stack.2
  159.5 374.9 %all_to_all.37 = bf16[64,8,8,1024]{3,2,1,0:T(8,128)(2,1)} all-to-all(bf16[64,8,8,1024]{3,2,1,0:T(8,128)(2,1)S(1)} %stack.2), channel_id=1, replica_groups=mesh['doc'=64,'bin'=8] {'doc'}, dimensions={0} | all-to-all | bytes 16777216 | tf_op jit(solution)/shard_map/all_to_all | solution.py:52
  534.4 0.0 copy-start
  534.4 8.1 %copy.5 = bf16[64,8,8,1024]{3,2,0,1:T(8,128)(2,1)} copy(bf16[64,8,8,1024]{3,2,1,0:T(8,128)(2,1)} %all_to_all.37) | data formatting | bytes 16777216 | tf_op jit(solution)/shard_map/all_to_all | solution.py:52
  542.5 0.0 copy-done
  542.5 7.1 %fusion.4 = f32[4096,128]{1,0:T(8,128)} fusion(bf16[4096,1024]{1,0:T(8,128)(2,1)} %bitcast.20, f32[128,1024]{1,0:T(8,128)S(1)} %copy-done), kind=kOutput, calls=%fused_computation.6 | convolution fusion | flops 1073872896 | bytes 11010048 | tf_op jit(solution)/shard_map/dot_general | solution.py:57
  549.6 0.0 reduce-scatter.2.cloned.1.call-update
  549.7 9.9 %all_to_all.38 = f32[8,8,1024]{2,1,0:T(8,128)S(1)} all-to-all(f32[8,8,1024]{2,1,0:T(8,128)S(1)} %get-tuple-element.3), channel_id=1, replica_groups=mesh['doc'=64,'bin'=8] {'bin'}, dimensions={0} | all-to-all | bytes 524288 | tf_op jit(solution)/shard_map/all_to_all | solution.py:48
  559.6 23.8 %reduce-scatter.2.cloned.1.call-done = f32[512,128]{1,0:T(8,128)} async-done(((f32[4096,128]{1,0:T(8,128)}), f32[512,128]{1,0:T(8,128)}) %reduce-scatter.2.cloned.1.call-update) | async-done | bytes 262160 | tf_op jit(solution)/shard_map/reduce_scatter | solution.py:56
  583.4 0.7 copy.7
  (3 shorter events, 0.0 us)
Async XLA Ops:
  10.0 32.2 %all-to-all-start = ((s32[64,1,8]{2,1,0:T(1,128)}), s32[64,1,8]{2,1,0:T(1,128)S(1)}, u32[]{:S(2)}, u32[]{:S(2)}) async-start(s32[64,1,8]{2,1,0:T(1,128)} %bitcast), calls=%async_computation | async-start | bytes 65536 | tf_op jit(solution)/shard_map/all_to_all | solution.py:33
  42.2 102.7 %all-to-all-start.1 = ((f32[64,8,1024]{2,1,0:T(8,128)}), f32[64,8,1024]{2,1,0:T(8,128)S(1)}, u32[]{:S(2)}, u32[]{:S(2)}) async-start(f32[64,8,1024]{2,1,0:T(8,128)} %bitcast.1), calls=%async_computation.1 | async-start | bytes 4194304 | tf_op jit(solution)/shard_map/all_to_all | solution.py:32
  47.8 535.7 %reduce-scatter.2.cloned.1.call-start = ((), (), s32[]{:S(2)}) async-start(), calls=%async_computation.5 | async-start | bytes 2359296 | tf_op jit(solution)/shard_map/reduce_scatter | solution.py:56
  534.4 8.1 %copy-start = (f32[128,1024]{1,0:T(8,128)S(1)}, f32[128,1024]{1,0:T(8,128)}, u32[]{:S(2)}) copy-start(f32[128,1024]{1,0:T(8,128)} %param.2) | copy-start | bytes 1572868
Sparse Core Ops, SparseCore 0:
  549.8 33.6 reduce-scatter.1
